TPU v7x, 32 devices: a whole 2x2x4 slice. The times are simulated.
32 devices in a mesh: sim: 8 (over y, x, core), section: 4 (over z).
Axes of the slice: x: 2, y: 2, z: 4, core: 2. Of those that a mesh axis runs over, the one named last changes fastest.
Arguments:
- density: float32 [4, 768, 512], P(None, 'sim', 'section'), may hold values from 0.5 to 2
- momentum: float32 [3, 4, 768, 512], P(None, None, 'sim', 'section'), may hold values from -1 to 1
- energy: float32 [4, 768, 512], P(None, 'sim', 'section'), may hold values from 4 to 8
- membership: int32 [192, 128], P(('sim', 'section')), may hold values from 0 to 63
- slot_of_brick: int32 [8, 4], P('sim'), may hold values from 0 to 3, each once within a row
Outputs:
- coded: float32 [5, 4, 768, 512], P(None, None, ('sim', 'section'))
- group_peak: float32 [5, 64], replicated
Inputs may be any that keep to these rules, and one draw needn't show every extreme that they name: `slot_of_brick`: each row is a permutation of the 4 bricks.
All inputs are finite; a program needn't handle non-finite values.
Results may differ from a plain program's by a relative error of at most 0.0003.
Values sent between devices are 32-bit elements; how exact they have to be, the bound alone decides.
No kernel may reach another device: no remote copies, remote signals or barrier semaphores. Data moves between devices by JAX's collectives and lax.ppermute only.
A program may use at most 64 MiB of HBM per device.

v0:
```python
import jax
import jax.numpy as jnp
from jax import lax
from jax.sharding import PartitionSpec as P

GAMMA_LESS = 0.4
COURANT = 0.05
DIFFUSE = 0.1
EPSILON = 1e-06
HIGH = lax.Precision.HIGHEST


def with_halo(block, sides, width):
    for axis, dim in sides:
        count = lax.axis_size(axis)
        forward = [(i, i + 1) for i in range(count - 1)]
        forward.append((count - 1, 0))
        backward = [(target, source) for source, target in forward]
        low = lax.ppermute(
            lax.slice_in_dim(block, block.shape[dim] - width, None, axis=dim), axis, forward
        )
        high = lax.ppermute(lax.slice_in_dim(block, 0, width, axis=dim), axis, backward)
        block = jnp.concatenate([low, block, high], axis=dim)
    return block


def flux_update(padded):
    density_c = padded[0]
    momentum_x = padded[1]
    momentum_y = padded[2]
    momentum_z = padded[3]
    energy_c = padded[4]
    velocity_x = momentum_x / density_c
    velocity_y = momentum_y / density_c
    kinetic = (
        0.5
        * (momentum_x * momentum_x + momentum_y * momentum_y + momentum_z * momentum_z)
        / density_c
    )
    pressure = GAMMA_LESS * (energy_c - kinetic)
    flux_x = jnp.stack(
        [
            momentum_x,
            momentum_x * velocity_x + pressure,
            momentum_y * velocity_x,
            momentum_z * velocity_x,
            (energy_c + pressure) * velocity_x,
        ]
    )
    flux_y = jnp.stack(
        [
            momentum_y,
            momentum_x * velocity_y,
            momentum_y * velocity_y + pressure,
            momentum_z * velocity_y,
            (energy_c + pressure) * velocity_y,
        ]
    )
    center = padded[:, :, 1:-1, 1:-1]
    spread = (
        padded[:, :, 1:-1, 2:]
        + padded[:, :, 1:-1, :-2]
        + padded[:, :, 2:, 1:-1]
        + padded[:, :, :-2, 1:-1]
        - 4.0 * center
    )
    return (
        center
        - COURANT * (flux_x[:, :, 1:-1, 2:] - flux_x[:, :, 1:-1, :-2])
        - COURANT * (flux_y[:, :, 2:, 1:-1] - flux_y[:, :, :-2, 1:-1])
        + DIFFUSE * spread
    )


def predict(extended):
    h = extended.shape[2] - 6
    guess = (
        -extended[:, :, 0:h]
        + 9.0 * extended[:, :, 2 : h + 2]
        + 9.0 * extended[:, :, 4 : h + 4]
        - extended[:, :, 6 : h + 6]
    ) / 16.0
    return extended[:, :, 3 : h + 3] - guess


def cosine_entry(k, d):
    factor = jnp.where(k == 0, 0.5, jnp.sqrt(0.5))
    return factor * jnp.cos(jnp.pi * (2.0 * d + 1.0) * k / 8.0)


def cosines():
    k = jnp.arange(4, dtype=jnp.float32)[:, None]
    m = jnp.arange(4, dtype=jnp.float32)[None, :]
    return cosine_entry(k, m)


def brick_matrix(brick_width):
    quarter = brick_width // 4
    m = jnp.arange(brick_width, dtype=jnp.int32)[:, None]
    column = jnp.arange(brick_width, dtype=jnp.int32)[None, :]
    k = column // quarter
    j = column % quarter
    d = m - 4 * j
    entries = cosine_entry(k.astype(jnp.float32), jnp.clip(d, 0, 3).astype(jnp.float32))
    return jnp.where((d >= 0) & (d < 4), entries, 0.0)


def transform(residual, brick_width):
    f, z, y, x = residual.shape
    along_z = jnp.einsum("kz,fzyx->fkyx", cosines(), residual, precision=HIGH)
    blocked = along_z.reshape(f, z, y // 4, 4, x)
    along_y = jnp.einsum("km,fzbmx->fzbkx", cosines(), blocked, precision=HIGH).reshape(f, z, y, x)
    bricks = along_y.reshape(f, z, y, x // brick_width, brick_width)
    return jnp.einsum("fzybm,mc->fzybc", bricks, brick_matrix(brick_width), precision=HIGH).reshape(
        f, z, y, x
    )


def reorder(coefficients, slot_of_brick, brick_width):
    f, z, y, x = coefficients.shape
    count = x // brick_width
    slabs = slot_of_brick.shape[0]
    placing = (
        slot_of_brick[:, :, None] == jnp.arange(count, dtype=jnp.int32)[None, None, :]
    ).astype(jnp.float32)
    bricks = coefficients.reshape(f, z, slabs, y // slabs, count, brick_width)
    return jnp.einsum("sbp,fzsybx->fzsypx", placing, bricks, precision=HIGH).reshape(f, z, y, x)


def block_peaks(coefficients, brick_width):
    f, z, y, x = coefficients.shape
    magnitude = jnp.max(jnp.abs(coefficients), axis=1)
    magnitude = jnp.max(magnitude.reshape(f, y // 4, 4, x), axis=2)
    magnitude = magnitude.reshape(f, y // 4, x // brick_width, 4, brick_width // 4)
    return jnp.max(magnitude, axis=3).reshape(f, y // 4, x // 4)


def gather_peaks(peaks, membership, groups):
    labels = jnp.arange(groups, dtype=jnp.int32)

    def gather_visit(carry, row):
        row_peaks, row_labels = row
        matches = row_labels[:, None] == labels[None, :]
        found = jnp.max(jnp.where(matches[None], row_peaks[:, :, None], 0.0), axis=1)
        return (jnp.maximum(carry, found), None)

    start = jnp.zeros((peaks.shape[0], groups), jnp.float32)
    result, unused = lax.scan(gather_visit, start, (jnp.moveaxis(peaks, 1, 0), membership))
    return result


def spread_peaks(group_peak, membership):
    labels = jnp.arange(group_peak.shape[1], dtype=jnp.int32)

    def spread_visit(row_labels):
        matches = (row_labels[:, None] == labels[None, :]).astype(jnp.float32)
        return jnp.dot(group_peak, matches.T, precision=HIGH)

    return jnp.moveaxis(lax.map(spread_visit, membership), 0, 1)


def normalize(coefficients, divisor, brick_width):
    f, z, y, x = coefficients.shape
    rows_count = y // 4
    widened = divisor.reshape(f, rows_count, x // brick_width, 1, brick_width // 4)
    widened = jnp.broadcast_to(
        widened, (f, rows_count, x // brick_width, 4, brick_width // 4)
    ).reshape(f, rows_count, x)
    widened = jnp.broadcast_to(widened[:, None, :, None, :], (f, z, rows_count, 4, x)).reshape(
        f, z, y, x
    )
    return coefficients / (widened + EPSILON)


def relay_slabs(blocks):
    return lax.all_to_all(blocks, "section", split_axis=2, concat_axis=3, tiled=True)


def shallow_update(conserved):
    padded = with_halo(conserved, (("sim", 2), ("section", 3)), 1)
    return flux_update(padded)


def per_device(density, momentum, energy, membership, slot_of_brick):
    conserved = jnp.concatenate([density[None], momentum, energy[None]], axis=0)
    brick_width = conserved.shape[3]
    updated = shallow_update(conserved)
    extended = with_halo(updated, (("sim", 2),), 3)
    transformed = relay_slabs(transform(predict(extended), brick_width))
    placed = reorder(transformed, slot_of_brick, brick_width)
    peaks = block_peaks(placed, brick_width)
    groups = 2 * lax.axis_size("sim") * lax.axis_size("section")
    local_peak = gather_peaks(peaks, membership, groups)
    group_peak = lax.pmax(local_peak, ("sim", "section"))
    coded = normalize(placed, spread_peaks(group_peak, membership), brick_width)
    return (coded, group_peak)


def solution(mesh):
    placed = (
        P(None, "sim", "section"),
        P(None, None, "sim", "section"),
        P(None, "sim", "section"),
        P(("sim", "section"), None),
        P("sim", None),
    )
    return jax.shard_map(
        per_device,
        mesh=mesh,
        in_specs=placed,
        out_specs=(P(None, None, ("sim", "section"), None), P()),
        check_vma=False,
    )
```

profile of v0, /device:TPU:0, one launch (start us, length us, event | category | flops | bytes accessed | tf_op | source)
XLA Modules:
  0.0 128.9 jit_solution(9502653264941293681)
XLA Ops:
  0.6 1.3 pad_maximum_fusion.11
  1.9 0.5 collective-permute-start
  2.5 3.0 %collective-permute-start.1 = (f32[5,4,1,128]{3,0,2,1:T(8,128)S(1)}, f32[5,4,1,128]{3,0,2,1:T(8,128)S(1)}, u32[]{:S(2)}, u32[]{:S(2)}) collective-permute-start(f32[5,4,1,128]{3,0,2,1:T(8,128)S(1)} %copy.114), channel_id=1, source_target_pairs={{4,0},{8,4},{12,8},{16,12},{20,16},{24,20},{28,24},{0,28},{5,1},{9... | collective-permute-start | bytes 30728 | tf_op jit(solution)/shard_map/ppermute | solution.py:22
  5.4 0.4 copy.87
  5.8 0.9 collective-permute-done
  6.8 0.4 copy.80
  7.2 1.5 %copy.82 = f32[5,4,1,128]{2,3,1,0:T(8,128)} copy(f32[5,4,1,128]{3,0,2,1:T(8,128)S(1)} %collective-permute-done.1) | data formatting | bytes 20480 | tf_op jit(solution)/shard_map/ppermute | solution.py:22
  8.7 1.2 pad_maximum_fusion.12
  9.9 2.4 %collective-permute-start.2 = (f32[5,4,98,1]{2,0,3,1:T(8,128)S(1)}, f32[5,4,98,1]{2,0,3,1:T(8,128)S(1)}, u32[]{:S(2)}, u32[]{:S(2)}) collective-permute-start(f32[5,4,98,1]{2,0,3,1:T(8,128)S(1)} %copy.83), channel_id=1, source_target_pairs={{0,1},{1,2},{2,3},{3,0},{4,5},{5,6},{6,7},{7,4},{8,9},{9,10},{10,1... | collective-permute-start | bytes 23528 | tf_op jit(solution)/shard_map/ppermute | solution.py:19
  12.3 2.1 %collective-permute-start.3 = (f32[5,4,98,1]{2,0,3,1:T(8,128)S(1)}, f32[5,4,98,1]{2,0,3,1:T(8,128)S(1)}, u32[]{:S(2)}, u32[]{:S(2)}) collective-permute-start(f32[5,4,98,1]{2,0,3,1:T(8,128)S(1)} %copy.84), channel_id=1, source_target_pairs={{1,0},{2,1},{3,2},{0,3},{5,4},{6,5},{7,6},{4,7},{9,8},{10,9},{11,1... | collective-permute-start | bytes 23528 | tf_op jit(solution)/shard_map/ppermute | solution.py:22
  14.4 1.7 %collective-permute-done.2 = f32[5,4,98,1]{2,0,3,1:T(8,128)S(1)} collective-permute-done((f32[5,4,98,1]{2,0,3,1:T(8,128)S(1)}, f32[5,4,98,1]{2,0,3,1:T(8,128)S(1)}, u32[]{:S(2)}, u32[]{:S(2)}) %collective-permute-start.2) | collective-permute-done | bytes 7872 | tf_op jit(solution)/shard_map/ppermute | solution.py:19
  16.3 0.8 pad_maximum_fusion
  17.6 1.2 copy-done.1
  18.8 3.9 %fusion.16 = f32[5,4,96,128]{2,3,1,0:T(8,128)S(1)} fusion(f32[5,4,96,128]{2,3,1,0:T(8,128)S(1)} %copy.87, f32[5,4,1,128]{2,3,1,0:T(8,128)S(1)} %copy-done.1, f32[5,4,1,128]{2,3,1,0:T(8,128)S(1)} %copy-done.2, f32[5,4,98,1]{2,3,1,0:T(1,128)S(1)} %copy.85, f32[5,4,98,1]{2,3,1,0:T(1,128)S(1)} %copy.86, ...), kind=kLoop, calls=%fused_computation.30 | loop fusion | flops 5160960 | bytes 5934400 | tf_op jit(solution)/shard_map/add | solution.py:68
  22.7 1.5 %fusion.76 = (f32[5,4,3,128]{2,3,1,0:T(8,128)}, f32[5,4,3,128]{2,3,1,0:T(8,128)S(1)}) fusion(f32[5,4,96,128]{2,3,1,0:T(8,128)S(1)} %fusion.16), kind=kLoop, calls=%fused_computation.129 | loop fusion | bytes 122880 | tf_op jit(solution)/shard_map/slice | solution.py:20
  24.3 1.9 %copy.95 = f32[5,4,3,128]{3,0,2,1:T(8,128)S(1)} copy(f32[5,4,3,128]{2,3,1,0:T(8,128)} %get-tuple-element.136) | data formatting | bytes 61440 | tf_op jit(solution)/shard_map/slice | solution.py:20
  26.2 0.6 copy.97
  26.9 2.8 %collective-permute-start.5 = (f32[5,4,3,128]{3,0,2,1:T(8,128)S(1)}, f32[5,4,3,128]{3,0,2,1:T(8,128)S(1)}, u32[]{:S(2)}, u32[]{:S(2)}) collective-permute-start(f32[5,4,3,128]{3,0,2,1:T(8,128)S(1)} %copy.97), channel_id=1, source_target_pairs={{4,0},{8,4},{12,8},{16,12},{20,16},{24,20},{28,24},{0,28},{5,1},{9... | collective-permute-start | bytes 92168 | tf_op jit(solution)/shard_map/ppermute | solution.py:22
  29.7 0.9 collective-permute-done.4
  30.6 0.4 copy.96
  31.1 0.4 collective-permute-done.5
  31.5 1.5 %copy.98 = f32[5,4,3,128]{2,3,1,0:T(8,128)} copy(f32[5,4,3,128]{3,0,2,1:T(8,128)S(1)} %collective-permute-done.5) | data formatting | bytes 61440 | tf_op jit(solution)/shard_map/ppermute | solution.py:22
  33.0 5.2 %fusion.9 = f32[5,4,96,128]{2,3,1,0:T(8,128)} fusion(f32[5,4,96,128]{2,3,1,0:T(8,128)S(1)} %fusion.16, f32[5,4,3,128]{2,3,1,0:T(8,128)} %copy.98, f32[5,4,3,128]{2,3,1,0:T(8,128)S(1)} %copy.96), kind=kLoop, calls=%fused_computation.19 | loop fusion | flops 2949120 | bytes 2027520 | tf_op jit(solution)/shard_map/sub | solution.py:83
  38.2 2.0 %copy.99 = f32[5,4,96,128]{3,1,2,0:T(4,128)S(1)} copy(f32[5,4,96,128]{2,3,1,0:T(8,128)} %fusion.9) | data formatting | bytes 1966080 | tf_op jit(solution)/shard_map/sub | solution.py:83
  40.3 1.8 %fusion.54 = f32[5,96,128,4]{2,3,1,0:T(4,128)S(1)} fusion(f32[5,4,96,128]{3,1,2,0:T(4,128)S(1)} %copy.99, f32[4]{0:T(128)S(1)} %get-tuple-element.143, f32[4]{0:T(128)S(1)} %get-tuple-element.142), kind=kOutput, calls=%fused_computation.97 | convolution fusion | flops 11796528 | bytes 1966112 | tf_op jit(solution)/shard_map/kz,fzyx->fkyx/dot_general | solution.py:110
  42.1 1.8 %fusion.25 = f32[5,4,24,128,4]{3,4,2,1,0:T(4,128)S(1)} fusion(f32[5,4,24,4,128]{4,1,3,2,0:T(4,128)S(1)} %bitcast.72, f32[4]{0:T(128)S(1)} %get-tuple-element.143, f32[4]{0:T(128)S(1)} %get-tuple-element.142), kind=kOutput, calls=%fused_computation.49 | convolution fusion | flops 11796528 | bytes 1966112 | tf_op jit(solution)/shard_map/km,fzbmx->fzbkx/dot_general | solution.py:112
  44.0 1.2 fusion.27
  45.1 1.6 %copy.101 = f32[5,4,96,128]{3,1,0,2:T(4,128)} copy(f32[5,4,96,128]{3,2,1,0:T(8,128)S(1)} %fusion.27) | data formatting | bytes 1966080 | tf_op jit(solution)/shard_map/fzybm,mc->fzybc/dot_general | solution.py:114
  46.7 5.1 %all-to-all-start = ((f32[5,4,96,128]{3,1,0,2:T(4,128)}), f32[5,4,96,128]{3,1,0,2:T(4,128)S(1)}, u32[]{:S(2)}, u32[]{:S(2)}) async-start(f32[5,4,96,128]{3,1,0,2:T(4,128)} %copy.101), calls=%async_computation | async-start | bytes 1966080 | tf_op jit(solution)/shard_map/all_to_all | solution.py:176
  51.8 24.5 %all-to-all-done = f32[5,4,96,128]{3,1,0,2:T(4,128)S(1)} async-done(((f32[5,4,96,128]{3,1,0,2:T(4,128)}), f32[5,4,96,128]{3,1,0,2:T(4,128)S(1)}, u32[]{:S(2)}, u32[]{:S(2)}) %all-to-all-start) | async-done | bytes 983072 | tf_op jit(solution)/shard_map/all_to_all | solution.py:176
  76.3 1.8 %abs_reduce_fusion = (f32[5,24,4,128]{3,2,1,0:T(4,128)S(1)}, f32[5,4,1,24,4,128]{5,4,3,1,0,2:T(4,128)S(1)}) fusion(s32[4]{0:T(128)S(1)} %bitcast.79, f32[5,4,4,24,128]{4,1,0,3,2:T(4,128)S(1)} %bitcast.73), kind=kOutput, calls=%fused_computation.51 | convolution fusion | flops 12226576 | bytes 2211856 | tf_op jit(solution)/shard_map/sbp,fzsybx->fzsypx/dot_general | solution.py:127
  78.8 5.3 %while.23 = (s32[]{:T(128)}, f32[5,64]{1,0:T(8,128)S(1)}, s32[6,128]{1,0:T(8,128)}, f32[6,5,128]{2,0,1:T(8,128)S(1)}, s32[]{:T(128)}, /*index=5*/s32[]{:T(128)}) while((s32[]{:T(128)}, f32[5,64]{1,0:T(8,128)S(1)}, s32[6,128]{1,0:T(8,128)}, f32[6,5,128]{2,0,1:T(8,128)S(1)}, s32[]{:T(128)}, /*index=5*/s32[]{:T(128)}) %tuple.65), condition=%wide.region_5.6_spmd.clone, body=%wide.region_3.5_spmd.clone.sunk | while | flops 90435 | bytes 35927 | solution.py:148
  78.8 0.7 dynamic-slice_bitcast_fusion.2
  79.7 0.7 dynamic-slice_bitcast_fusion.2
  80.6 0.7 dynamic-slice_bitcast_fusion.2
  81.5 0.7 dynamic-slice_bitcast_fusion.2
  82.4 0.7 dynamic-slice_bitcast_fusion.2
  83.3 0.7 dynamic-slice_bitcast_fusion.2
  84.2 37.0 %pmax.7 = f32[5,64]{1,0:T(8,128)S(1)} all-reduce(f32[5,64]{1,0:T(8,128)S(1)} %get-tuple-element.56), channel_id=1, replica_groups=mesh['sim'=8,'section'=4] {'sim','section'}, use_global_device_ids=true, to_apply=%region_6.7 | all-reduce | flops 320 | bytes 2560 | tf_op jit(solution)/shard_map/pmax | solution.py:194
  121.2 5.6 %while.22 = (s32[]{:T(128)}, f32[6,5,128]{2,1,0:T(8,128)S(1)}, s32[6,128]{1,0:T(8,128)}, f32[5,64]{1,0:T(8,128)S(1)}, s32[]{:T(128)}) while((s32[]{:T(128)}, f32[6,5,128]{2,1,0:T(8,128)S(1)}, s32[6,128]{1,0:T(8,128)}, f32[5,64]{1,0:T(8,128)S(1)}, s32[]{:T(128)}) %tuple.66), condition=%wide.region_8.9_spmd.clone, body=%wide.region_7.8_spmd.clone.sunk | while | flops 499714 | bytes 9797 | solution.py:159
  121.2 0.7 fusion.85
  122.0 0.8 fusion.85
  123.0 0.8 fusion.85
  124.0 0.8 fusion.85
  124.9 0.8 fusion.85
  125.9 0.8 fusion.85
  127.4 0.4 reshape.190
  127.8 1.1 broadcast_divide_fusion
  (80 shorter events, 3.9 us)
Async XLA Ops:
  1.9 4.8 %collective-permute-start = (f32[5,4,1,128]{3,0,2,1:T(8,128)S(1)}, f32[5,4,1,128]{3,0,2,1:T(8,128)S(1)}, u32[]{:S(2)}, u32[]{:S(2)}) collective-permute-start(f32[5,4,1,128]{3,0,2,1:T(8,128)S(1)} %copy.113), channel_id=1, source_target_pairs={{0,4},{4,8},{8,12},{12,16},{16,20},{20,24},{24,28},{28,0},{1,5},{5... | collective-permute-start | bytes 30728 | tf_op jit(solution)/shard_map/ppermute | solution.py:19
  2.5 4.8 %collective-permute-start.1 = (f32[5,4,1,128]{3,0,2,1:T(8,128)S(1)}, f32[5,4,1,128]{3,0,2,1:T(8,128)S(1)}, u32[]{:S(2)}, u32[]{:S(2)}) collective-permute-start(f32[5,4,1,128]{3,0,2,1:T(8,128)S(1)} %copy.114), channel_id=1, source_target_pairs={{4,0},{8,4},{12,8},{16,12},{20,16},{24,20},{28,24},{0,28},{5,1},{9... | collective-permute-start | bytes 30728 | tf_op jit(solution)/shard_map/ppermute | solution.py:22
  7.2 9.1 %copy-start = (f32[5,4,1,128]{2,3,1,0:T(8,128)}, f32[5,4,1,128]{2,3,1,0:T(8,128)S(1)}, u32[]{:S(2)}) copy-start(f32[5,4,1,128]{2,3,1,0:T(8,128)S(1)} %copy.80) | copy-start | bytes 30724
  8.7 7.5 %copy-start.2 = (f32[5,4,1,128]{2,3,1,0:T(8,128)S(1)}, f32[5,4,1,128]{2,3,1,0:T(8,128)}, u32[]{:S(2)}) copy-start(f32[5,4,1,128]{2,3,1,0:T(8,128)} %copy.82) | copy-start | bytes 30724
  9.9 6.2 %collective-permute-start.2 = (f32[5,4,98,1]{2,0,3,1:T(8,128)S(1)}, f32[5,4,98,1]{2,0,3,1:T(8,128)S(1)}, u32[]{:S(2)}, u32[]{:S(2)}) collective-permute-start(f32[5,4,98,1]{2,0,3,1:T(8,128)S(1)} %copy.83), channel_id=1, source_target_pairs={{0,1},{1,2},{2,3},{3,0},{4,5},{5,6},{6,7},{7,4},{8,9},{9,10},{10,1... | collective-permute-start | bytes 23528 | tf_op jit(solution)/shard_map/ppermute | solution.py:19
  12.3 3.9 %collective-permute-start.3 = (f32[5,4,98,1]{2,0,3,1:T(8,128)S(1)}, f32[5,4,98,1]{2,0,3,1:T(8,128)S(1)}, u32[]{:S(2)}, u32[]{:S(2)}) collective-permute-start(f32[5,4,98,1]{2,0,3,1:T(8,128)S(1)} %copy.84), channel_id=1, source_target_pairs={{1,0},{2,1},{3,2},{0,3},{5,4},{6,5},{7,6},{4,7},{9,8},{10,9},{11,1... | collective-permute-start | bytes 23528 | tf_op jit(solution)/shard_map/ppermute | solution.py:22
  17.5 1.3 %copy-start.1 = (f32[5,4,1,128]{2,3,1,0:T(8,128)S(1)}, f32[5,4,1,128]{2,3,1,0:T(8,128)}, u32[]{:S(2)}) copy-start(f32[5,4,1,128]{2,3,1,0:T(8,128)} %copy-done) | copy-start | bytes 30724
  26.2 4.4 %collective-permute-start.4 = (f32[5,4,3,128]{3,0,2,1:T(8,128)S(1)}, f32[5,4,3,128]{3,0,2,1:T(8,128)S(1)}, u32[]{:S(2)}, u32[]{:S(2)}) collective-permute-start(f32[5,4,3,128]{3,0,2,1:T(8,128)S(1)} %copy.95), channel_id=1, source_target_pairs={{0,4},{4,8},{8,12},{12,16},{16,20},{20,24},{24,28},{28,0},{1,5},{5... | collective-permute-start | bytes 92168 | tf_op jit(solution)/shard_map/ppermute | solution.py:19
  26.9 4.6 %collective-permute-start.5 = (f32[5,4,3,128]{3,0,2,1:T(8,128)S(1)}, f32[5,4,3,128]{3,0,2,1:T(8,128)S(1)}, u32[]{:S(2)}, u32[]{:S(2)}) collective-permute-start(f32[5,4,3,128]{3,0,2,1:T(8,128)S(1)} %copy.97), channel_id=1, source_target_pairs={{4,0},{8,4},{12,8},{16,12},{20,16},{24,20},{28,24},{0,28},{5,1},{9... | collective-permute-start | bytes 92168 | tf_op jit(solution)/shard_map/ppermute | solution.py:22
  46.7 29.6 %copy-start.4 = (s32[1,4]{1,0:T(1,128)S(1)}, s32[1,4]{1,0:T(1,128)}, u32[]{:S(2)}) copy-start(s32[1,4]{1,0:T(1,128)} %param.13) | copy-start | bytes 52
  46.7 29.6 %all-to-all-start = ((f32[5,4,96,128]{3,1,0,2:T(4,128)}), f32[5,4,96,128]{3,1,0,2:T(4,128)S(1)}, u32[]{:S(2)}, u32[]{:S(2)}) async-start(f32[5,4,96,128]{3,1,0,2:T(4,128)} %copy.101), calls=%async_computation | async-start | bytes 1966080 | tf_op jit(solution)/shard_map/all_to_all | solution.py:176
  126.8 1.0 copy-start.3
where the time goes:
time: 130 us; the launch traced here: 129 us
  blocking collectives  37 us (28%)
  waiting for transfers between devices  28.5 us (22%)
  local copies, waits for them, and re-layouts  23.4 us (18%)
  starting transfers between devices  15.9 us (12%)
  other arithmetic  15.1 us (12%)
  matrix products  7.76 us (6%)
    pmax x1, blocking collectives, per_device(): group_peak = lax.pmax(local_peak, ('sim', 'section'))  37 us
    all_to_all x1, waiting for transfers between devices, relay_slabs(): lax.all_to_all(blocks, 'section', split_axis=2, concat_axis=3, tiled=True)  24.5 us
    ppermute x3, starting transfers between devices, with_halo(): lax.ppermute(lax.slice_in_dim(block, 0, width, axis=dim), axis, backward)  7.89 us
    sub x1, other arithmetic, predict(): return extended[:, :, 3:h + 3] - guess  5.22 us
    all_to_all x1, starting transfers between devices, relay_slabs(): lax.all_to_all(blocks, 'section', split_axis=2, concat_axis=3, tiled=True)  5.12 us
    eq x6, local copies, waits for them, and re-layouts, spread_visit(): matches = (row_labels[:, None] == labels[None, :]).astype(jnp.float32)  4.49 us
    eq x6, local copies, waits for them, and re-layouts, gather_visit(): matches = row_labels[:, None] == labels[None, :]  4.17 us
    add x1, other arithmetic, flux_update(): center - COURANT * (flux_x[:, :, 1:-1, 2:] - flux_x[:, :, 1:-1, :-2])  3.88 us
  transfers between devices with their start and end apart: 7, of which 6 were waited for; matrix products, arithmetic and copies ran while one was open for 1% of the time, Pallas kernels for 0%

commit v1 on v0

v1 whole, which is shorter than its diff:
```python
import functools

import jax
import jax.numpy as jnp
import numpy as np
from jax import lax
from jax.experimental import pallas as pl
from jax.experimental.pallas import tpu as pltpu
from jax.sharding import PartitionSpec as P

GAMMA_LESS = 0.4
COURANT = 0.05
DIFFUSE = 0.1
EPSILON = 1e-06
FIELDS = 5
PAD = 8
LANES = 128
EVEN = 0.5
WIDE = float(np.sqrt(0.5) * np.cos(np.pi / 8))
NARROW = float(np.sqrt(0.5) * np.cos(3 * np.pi / 8))
VMEM_LIMIT = 48 * 1024 * 1024


def vmem():
    return pl.BlockSpec(memory_space=pltpu.VMEM)


def smem():
    return pl.BlockSpec(memory_space=pltpu.SMEM)


def lanes_of(shape):
    return lax.broadcasted_iota(jnp.int32, shape, 1)


def butterfly(a, b, c, d):
    s, t, u, v = a + d, b + c, a - d, b - c
    return (
        EVEN * (s + t),
        WIDE * u + NARROW * v,
        EVEN * (s - t),
        NARROW * u - WIDE * v,
    )


def brick_matrix(width):
    quarter = width // 4
    m = np.arange(width)[:, None]
    column = np.arange(width)[None, :]
    k, d = column // quarter, m - 4 * (column % quarter)
    factor = np.where(k == 0, 0.5, np.sqrt(0.5))
    entries = factor * np.cos(np.pi * (2 * np.clip(d, 0, 3) + 1) * k / 8)
    return np.where((d >= 0) & (d < 4), entries, 0.0).astype(np.float32)


def split_matrix(width):
    full = brick_matrix(width)
    high = full.astype(jnp.bfloat16)
    low = (full - high.astype(np.float32)).astype(jnp.bfloat16)
    return np.block([[high, low], [high, np.zeros_like(low)]]).astype(jnp.bfloat16)


def pack_kernel(density, momentum, energy, first_x, last_x, first_y, last_y, tl, tr, bl, br):
    depth, y, width = density.shape
    quarter = y // 4
    planes = [density.at[z] for z in range(depth)]
    planes += [momentum.at[f, z] for f in range(3) for z in range(depth)]
    planes += [energy.at[z] for z in range(depth)]
    lane = lanes_of((y, width))
    first = jnp.zeros((y, width), jnp.float32)
    last = jnp.zeros((y, width), jnp.float32)
    for j, plane in enumerate(planes):
        value = plane[...]
        first = jnp.where(lane == j, pltpu.roll(value, j, 1) if j else value, first)
        last = jnp.where(lane == j, pltpu.roll(value, j + 1, 1), last)
        first_y[4 * j : 4 * j + 4, :] = plane[0:4, :]
        last_y[4 * j : 4 * j + 4, :] = plane[y - 4 : y, :]
    for column, out in ((first, first_x), (last, last_x)):
        packed = column[0:quarter]
        for c in range(1, 4):
            packed = packed + pltpu.roll(column[c * quarter : (c + 1) * quarter], 32 * c, 1)
        out[...] = packed
    tl[...] = first[0:8]
    tr[...] = last[0:8]
    bl[...] = first[y - 8 : y]
    br[...] = last[y - 8 : y]


def pack(density, momentum, energy):
    depth, y, width = density.shape
    rows = 4 * FIELDS * depth
    shapes = [(y // 4, width)] * 2 + [(rows, width)] * 2 + [(8, width)] * 4
    return pl.pallas_call(
        pack_kernel,
        out_shape=[jax.ShapeDtypeStruct(s, jnp.float32) for s in shapes],
        in_specs=[vmem()] * 3,
        out_specs=[vmem()] * 8,
        compiler_params=pltpu.CompilerParams(vmem_limit_bytes=VMEM_LIMIT),
    )(density, momentum, energy)


def fluxes(c):
    rho, mx, my, mz, e = c
    inverse = 1.0 / rho
    u, v = mx * inverse, my * inverse
    pressure = GAMMA_LESS * (e - 0.5 * (mx * mx + my * my + mz * mz) * inverse)
    total = e + pressure
    flux_x = (mx, mx * u + pressure, my * u, mz * u, total * u)
    flux_y = (my, mx * v, my * v + pressure, mz * v, total * v)
    return flux_x, flux_y


def partner_of(me, k, count):
    if count & (count - 1) == 0:
        return me ^ k
    return lax.rem(me + k, count)


def main_kernel(count, groups, *refs):
    (density, momentum, energy, top, bottom, left, right, tl, tr, bl, br, membership, slots, matrix), refs = refs[:14], refs[14:]
    outs, peaks, refs = refs[:count], refs[count], refs[count + 1 :]
    pad, across, down, up, edges, folded, split, coefficients, staged, blocks, packed, table, sems = refs
    depth, y, width = density.shape
    nb, quarter = y // 4, y // 4
    rows = y // count
    tall = y + 2 * PAD
    copies = []
    sources = [density, momentum.at[0], momentum.at[1], momentum.at[2], energy]
    for f, source in enumerate(sources):
        copies.append(
            pltpu.make_async_copy(source, pad.at[pl.ds(f * depth, depth), pl.ds(PAD, y), :], sems.at[f])
        )
    for copy in copies:
        copy.start()
    for j in range(FIELDS * depth):
        pad[j, PAD - 4 : PAD, :] = top[4 * j : 4 * j + 4, :]
        pad[j, PAD + y : PAD + y + 4, :] = bottom[4 * j : 4 * j + 4, :]
        pad[j, 0:4, :] = jnp.ones((4, width), jnp.float32)
        pad[j, PAD + y + 4 : tall, :] = jnp.ones((4, width), jnp.float32)

    for side, (column, above, below) in enumerate(((left, tl, bl), (right, tr, br))):
        parts = [above[...]]
        for c in range(4):
            value = column[...]
            parts.append(pltpu.roll(value, LANES - 32 * c, 1) if c else value)
        parts.append(below[...])
        own = jnp.concatenate(parts, axis=0)
        fields = [pltpu.roll(own, LANES - depth * f, 1) if f else own for f in range(FIELDS)]
        flux_x, unused = fluxes(fields)
        sign = COURANT if side == 0 else -COURANT
        for f in range(FIELDS):
            edges[side, f] = DIFFUSE * fields[f] + sign * flux_x[f]

    for copy in copies:
        copy.wait()

    step = 16
    lane = lanes_of((step, width))
    is_first, is_last = lane == 0, lane == width - 1

    def flux_rows(i, carry):
        r = pl.ds(pl.multiple_of(i * step, step), step)
        low = [edges[0, f, r, :] for f in range(FIELDS)]
        high = [edges[1, f, r, :] for f in range(FIELDS)]
        for z in range(depth):
            c = [pad[f * depth + z, r, :] for f in range(FIELDS)]
            flux_x, flux_y = fluxes(c)
            for f in range(FIELDS):
                j = f * depth + z
                base = DIFFUSE * c[f]
                gx, gy = COURANT * flux_x[f], COURANT * flux_y[f]
                from_left = pltpu.roll(base + gx, 1, 1)
                from_right = pltpu.roll(base - gx, width - 1, 1)
                at_left = pltpu.roll(low[f], LANES - z, 1) if z else low[f]
                at_right = pltpu.roll(high[f], LANES - 1 - z, 1)
                across[j, r, :] = (
                    (1.0 - 4.0 * DIFFUSE) * c[f]
                    + jnp.where(is_first, at_left, from_left)
                    + jnp.where(is_last, at_right, from_right)
                )
                down[j, r, :] = base + gy
                up[j, r, :] = base - gy
        return carry

    lax.fori_loop(0, tall // step, flux_rows, 0)

    def predict_rows(j, carry):
        t = {}
        for o in range(-3, 7):
            t[o] = (
                across[j, pl.ds(PAD + o, nb, stride=4), :]
                + down[j, pl.ds(PAD + o - 1, nb, stride=4), :]
                + up[j, pl.ds(PAD + o + 1, nb, stride=4), :]
            )
        residual = [
            t[m] - (9.0 / 16.0) * (t[m - 1] + t[m + 1]) + (1.0 / 16.0) * (t[m - 3] + t[m + 3])
            for m in range(4)
        ]
        for k, value in enumerate(butterfly(*residual)):
            folded[j, k * nb : (k + 1) * nb, :] = value
        return carry

    lax.fori_loop(0, FIELDS * depth, predict_rows, 0)

    piece = 32

    def transform_field(f, carry):
        for start in range(0, y, piece):
            planes = [folded[f * depth + z, start : start + piece, :] for z in range(4)]
            for k, value in enumerate(butterfly(*planes)):
                high = value.astype(jnp.bfloat16)
                low = (value - high.astype(jnp.float32)).astype(jnp.bfloat16)
                split[k * y + start : k * y + start + piece, 0:width] = high
                split[k * y + start : k * y + start + piece, width : 2 * width] = low
        product = jnp.dot(split[...], matrix[...], preferred_element_type=jnp.float32)
        result = product[:, 0:width] + product[:, width : 2 * width]
        peak = None
        for k in range(4):
            for m in range(4):
                value = result[k * y + m * nb : k * y + (m + 1) * nb]
                coefficients[f * depth + k, pl.ds(m, nb, stride=4), :] = value
                size = jnp.abs(value)
                peak = size if peak is None else jnp.maximum(peak, size)
        peak = jnp.maximum(peak, pltpu.roll(peak, 64, 1))
        blocks[f] = jnp.maximum(peak, pltpu.roll(peak, 32, 1))
        return carry

    lax.fori_loop(0, FIELDS, transform_field, 0)

    me = lax.axis_index("section")
    if rows % 8 == 0:
        for k in range(count):
            p = partner_of(me, k, count)
            for j in range(FIELDS * depth):
                outs[k][j // depth, j % depth] = coefficients[j, pl.ds(pl.multiple_of(p * rows, 8), rows), :]
    else:
        for p in range(count):
            staged[p] = coefficients[:, p * rows : (p + 1) * rows, :]
        for k in range(count):
            p = partner_of(me, k, count)
            for j in range(FIELDS * depth):
                outs[k][j // depth, j % depth] = staged[p, j]

    slot = slots[0, me]
    tile = membership[:, pl.ds(pl.multiple_of(lax.div(slot, 4) * LANES, LANES), LANES)]
    within = lax.rem(slot, 4) * 32
    sixth = nb // 4
    band = lax.div(lanes_of((sixth, LANES)), 32)
    labels = jnp.zeros((sixth, LANES), jnp.int32)
    for c in range(4):
        turned = pltpu.roll(tile, lax.rem(32 * c - within + LANES, LANES), 1)
        labels = jnp.where(band == c, turned[c * sixth : (c + 1) * sixth], labels)
    for f in range(FIELDS):
        own = jnp.zeros((sixth, LANES), jnp.float32)
        for c in range(4):
            own = jnp.where(band == c, blocks[f, c * sixth : (c + 1) * sixth, :], own)
        packed[f, 0:sixth, :] = own
    lane8 = lanes_of((8, LANES))
    sub8 = lax.broadcasted_iota(jnp.int32, (8, LANES), 0)
    label_rows = [jnp.broadcast_to(labels[r : r + 1], (8, LANES)) for r in range(sixth)]

    def group_tile(g, carry):
        wanted = sub8 + g * 8
        matches = [label_rows[r] == wanted for r in range(sixth)]
        found = jnp.zeros((8, LANES), jnp.float32)
        for f in range(FIELDS):
            best = jnp.zeros((8, LANES), jnp.float32)
            for r in range(sixth):
                row = jnp.broadcast_to(packed[f, r : r + 1, :], (8, LANES))
                best = jnp.maximum(best, jnp.where(matches[r], row, 0.0))
            found = jnp.where(lane8 == f, jnp.max(best, axis=1, keepdims=True), found)
        table[pl.ds(pl.multiple_of(g * 8, 8), 8), :] = found
        return carry

    high = table.shape[0]
    if groups < high:
        table[...] = jnp.zeros((high, LANES), jnp.float32)
    lax.fori_loop(0, pl.cdiv(groups, 8), group_tile, 0)
    for g in range(high // LANES):
        peaks[:, g * LANES : (g + 1) * LANES] = jnp.transpose(table[g * LANES : (g + 1) * LANES, :])[0:8]


def transform_bricks(count, groups, density, momentum, energy, halos, membership, slots):
    depth, y, width = density.shape
    rows = y // count
    planes, tall = FIELDS * depth, y + 2 * PAD
    high = pl.cdiv(groups, LANES) * LANES
    matrix = jnp.asarray(split_matrix(width))
    chunk = jax.ShapeDtypeStruct((FIELDS, depth, rows, width), jnp.float32)
    hbm = pl.BlockSpec(memory_space=pl.ANY)
    results = pl.pallas_call(
        functools.partial(main_kernel, count, groups),
        out_shape=[chunk] * count + [jax.ShapeDtypeStruct((8, high), jnp.float32)],
        in_specs=[hbm] * 3 + [vmem()] * 8 + [vmem(), smem(), vmem()],
        out_specs=[vmem()] * (count + 1),
        scratch_shapes=[
            pltpu.VMEM((planes, tall, width), jnp.float32),
            pltpu.VMEM((planes, tall, width), jnp.float32),
            pltpu.VMEM((planes, tall, width), jnp.float32),
            pltpu.VMEM((planes, tall, width), jnp.float32),
            pltpu.VMEM((2, FIELDS, tall, width), jnp.float32),
            pltpu.VMEM((planes, y, width), jnp.float32),
            pltpu.VMEM((depth * y, 2 * width), jnp.bfloat16),
            pltpu.VMEM((planes, y, width), jnp.float32),
            pltpu.VMEM((1, 1, 8, LANES) if rows % 8 == 0 else (count, planes, rows, width), jnp.float32),
            pltpu.VMEM((FIELDS, y // 4, width), jnp.float32),
            pltpu.VMEM((FIELDS, 8, LANES), jnp.float32),
            pltpu.VMEM((high, LANES), jnp.float32),
            pltpu.SemaphoreType.DMA((FIELDS,)),
        ],
        compiler_params=pltpu.CompilerParams(vmem_limit_bytes=VMEM_LIMIT),
    )(density, momentum, energy, *halos, membership, slots, matrix)
    return results[:count], results[count]


def scale_kernel(count, groups, *refs):
    chunks, (peaks, membership, slots, coded, group_peak, labels, wide) = refs[:count], refs[count:]
    fields, depth, rows, width = chunks[0].shape
    nb = rows // 4
    high = peaks.shape[1]
    me = lax.axis_index("section")
    group_peak[...] = peaks[0:fields, 0:groups]
    labels[...] = jnp.zeros(labels.shape, jnp.int32)
    labels[0:nb, :] = membership[...]
    lane = lanes_of((8, LANES))
    inverse = 1.0 / (peaks[...] + EPSILON)
    tables = [
        [jnp.broadcast_to(inverse[f : f + 1, g * LANES : (g + 1) * LANES], (8, LANES)) for g in range(high // LANES)]
        for f in range(fields)
    ]
    for k in range(count):
        slot = slots[0, partner_of(me, k, count) if k == 0 or count & (count - 1) == 0 else lax.rem(me - k + count, count)]
        tile = labels[:, pl.ds(pl.multiple_of(lax.div(slot, 4) * LANES, LANES), LANES)]
        within = lax.rem(slot, 4) * 32 + lax.rem(lane, 32)
        own = jnp.take_along_axis(tile, within, axis=1)
        place = pl.ds(pl.multiple_of(slot * width, width), width)
        for f in range(fields):
            if high == LANES:
                found = jnp.take_along_axis(tables[f][0], own, axis=1)
            else:
                found = jnp.zeros((8, LANES), jnp.float32)
                inside = lax.rem(own, LANES)
                for g in range(high // LANES):
                    here = jnp.take_along_axis(tables[f][g], inside, axis=1)
                    found = jnp.where(lax.div(own, LANES) == g, here, found)
            for m in range(4):
                wide[k, f, pl.ds(m, nb, stride=4), :] = found[0:nb]
            factor = wide[k, f]
            for z in range(depth):
                coded[f, z, :, place] = chunks[k][f, z] * factor


def scale(count, groups, chunks, peaks, membership, slots):
    fields, depth, rows, width = chunks[0].shape
    return pl.pallas_call(
        functools.partial(scale_kernel, count, groups),
        out_shape=[
            jax.ShapeDtypeStruct((fields, depth, rows, width * count), jnp.float32),
            jax.ShapeDtypeStruct((fields, groups), jnp.float32),
        ],
        in_specs=[vmem()] * (count + 2) + [smem()],
        out_specs=[vmem()] * 2,
        scratch_shapes=[
            pltpu.VMEM((8, membership.shape[1]), jnp.int32),
            pltpu.VMEM((count, fields, rows, width), jnp.float32),
        ],
        compiler_params=pltpu.CompilerParams(vmem_limit_bytes=VMEM_LIMIT),
    )(*chunks, peaks, membership, slots)


def ring(axis, shift):
    count = lax.axis_size(axis)
    return [(i, (i + shift) % count) for i in range(count)]


def diagonal(sim_shift, section_shift):
    n_sim, n_section = lax.axis_size("sim"), lax.axis_size("section")
    return [
        (s * n_section + b, (s + sim_shift) % n_sim * n_section + (b + section_shift) % n_section)
        for s in range(n_sim)
        for b in range(n_section)
    ]


def exchange_pairs(count, k):
    if count & (count - 1) == 0:
        return [(i, i ^ k) for i in range(count)]
    return [(i, (i + k) % count) for i in range(count)]


def largest(value, axis):
    count = lax.axis_size(axis)
    span = 1
    while span < count:
        shift = min(span, count - span)
        value = jnp.maximum(value, lax.ppermute(value, axis, exchange_pairs(count, shift)))
        span += shift
    return value


def per_device(density, momentum, energy, membership, slot_of_brick):
    count = lax.axis_size("section")
    groups = 2 * lax.axis_size("sim") * count
    slab_membership = lax.all_gather(membership, "section", axis=0, tiled=True)
    first_x, last_x, first_y, last_y, tl, tr, bl, br = pack(density, momentum, energy)
    both = ("sim", "section")
    halos = (
        lax.ppermute(last_y, "sim", ring("sim", 1)),
        lax.ppermute(first_y, "sim", ring("sim", -1)),
        lax.ppermute(last_x, "section", ring("section", 1)),
        lax.ppermute(first_x, "section", ring("section", -1)),
        lax.ppermute(br, both, diagonal(1, 1)),
        lax.ppermute(bl, both, diagonal(1, -1)),
        lax.ppermute(tr, both, diagonal(-1, 1)),
        lax.ppermute(tl, both, diagonal(-1, -1)),
    )
    chunks, peaks = transform_bricks(count, groups, density, momentum, energy, halos, slab_membership, slot_of_brick)
    moved = [chunks[0]] + [
        lax.ppermute(chunks[k], "section", exchange_pairs(count, k)) for k in range(1, count)
    ]
    peaks = largest(largest(peaks, "section"), "sim")
    return tuple(scale(count, groups, moved, peaks, membership, slot_of_brick))


def solution(mesh):
    placed = (
        P(None, "sim", "section"),
        P(None, None, "sim", "section"),
        P(None, "sim", "section"),
        P(("sim", "section"), None),
        P("sim", None),
    )
    return jax.shard_map(
        per_device,
        mesh=mesh,
        in_specs=placed,
        out_specs=(P(None, None, ("sim", "section"), None), P()),
        check_vma=False,
    )
```

time: 130 us -> 75.7 us (0.58)
  blocking collectives: 37 us -> 13.1 us
  local copies, waits for them, and re-layouts: 23.4 us -> 4.41 us
  other arithmetic: 15.1 us -> 0.02 us
  Pallas kernels: 0 us -> 8.6 us
  matrix products: 7.76 us -> 0 us
  starting transfers between devices: 15.9 us -> 22.3 us
  waiting for transfers between devices: 28.5 us -> 26.3 us
    pmax x1 -> x0, blocking collectives: 37 us -> none  [per_device(): group_peak = lax.pmax(local_peak, ('sim', 'section'))]
    all_to_all x1 -> x0, waiting for transfers between devices: 24.5 us -> none  [relay_slabs(): lax.all_to_all(blocks, 'section', split_axis=2, concat_axis=3, tiled=True)]
    ppermute x6 -> x16, waiting for transfers between devices: 4.03 us -> 26.3 us  [the longest x5 19.1 us: largest(): lax.ppermute(value, axis, exchange_pairs(count, shift))]
    all_gather x0 -> x1, blocking collectives: none -> 13.1 us  [per_device(): slab_membership = lax.all_gather(membership, 'section', axis=0, tiled=True)]
    ppermute x6 -> x16, starting transfers between devices: 10.8 us -> 22.3 us  [the longest x5 6.31 us: largest(): lax.ppermute(value, axis, exchange_pairs(count, shift))]
    eq x12 -> x0, local copies, waits for them, and re-layouts: 8.66 us -> none  [the longest x6 4.49 us: spread_visit(): matches = (row_labels[:, None] == labels[None, :]).astype(jnp.float32)]
    pallas_call x0 -> x3, Pallas kernels: none -> 8.6 us  [the longest x1 6.18 us: transform_bricks(): pl.pallas_call(functools.partial(main_kernel, count, groups), out_shape=[...]
    dot_general x10 -> x0, matrix products: 7.76 us -> none  [the longest x1 1.85 us: transform(): jnp.einsum('km,fzbmx->fzbkx', cosines(), blocked, precision=HIGH)]
  transfers between devices with their start and end apart: 7 -> 16, of which waited for: 6 -> 7; matrix products, arithmetic and copies ran while one was open for 1% -> 0% of each run, Pallas kernels for 0% -> 0%
where the time goes in v1:
time: 75.7 us; the launch traced here: 75.5 us
  waiting for transfers between devices  26.3 us (35%)
  starting transfers between devices  22.3 us (29%)
  blocking collectives  13.1 us (17%)
  Pallas kernels  8.6 us (11%)
  local copies, waits for them, and re-layouts  4.41 us (6%)
    ppermute x5, waiting for transfers between devices, largest(): lax.ppermute(value, axis, exchange_pairs(count, shift))  19.1 us
    all_gather x1, blocking collectives, per_device(): slab_membership = lax.all_gather(membership, 'section', axis=0, tiled=True)  13.1 us
    ppermute x5, starting transfers between devices, largest(): lax.ppermute(value, axis, exchange_pairs(count, shift))  6.31 us
    pallas_call x1, Pallas kernels, transform_bricks(): pl.pallas_call(functools.partial(main_kernel, count, groups), out_shape=[...  6.18 us
    ppermute x1, waiting for transfers between devices, per_device(): lax.ppermute(tr, both, diagonal(-1, 1))  4.83 us
    ppermute x3, starting transfers between devices, per_device(): lax.ppermute(chunks[k], 'section', exchange_pairs(count, k))  4.45 us
    unnamed x19, local copies, waits for them, and re-layouts  4.41 us
    ppermute x1, starting transfers between devices, per_device(): lax.ppermute(bl, both, diagonal(1, -1))  3.43 us
  transfers between devices with their start and end apart: 16, of which 7 were waited for; matrix products, arithmetic and copies ran while one was open for 0% of the time, Pallas kernels for 0%

profile of v1, /device:TPU:0, one launch (start us, length us, event | category | flops | bytes accessed | tf_op | source)
XLA Modules:
  0.0 75.5 jit_solution(12411688461102621301)
XLA Ops:
  0.6 0.0 copy-start
  0.6 1.1 %copy-done = f32[3,4,96,128]{3,2,1,0:T(8,128)S(1)} copy-done((f32[3,4,96,128]{3,2,1,0:T(8,128)S(1)}, f32[3,4,96,128]{3,2,1,0:T(8,128)}, u32[]{:S(2)}) %copy-start) | copy-done | bytes 589848
  1.7 0.0 copy-start.2
  1.7 0.9 %copy-done.2 = f32[4,96,128]{2,1,0:T(8,128)S(1)} copy-done((f32[4,96,128]{2,1,0:T(8,128)S(1)}, f32[4,96,128]{2,1,0:T(8,128)}, u32[]{:S(2)}) %copy-start.2) | copy-done | bytes 196632
  2.6 0.9 %copy-done.4 = f32[4,96,128]{2,1,0:T(8,128)S(1)} copy-done((f32[4,96,128]{2,1,0:T(8,128)S(1)}, f32[4,96,128]{2,1,0:T(8,128)}, u32[]{:S(2)}) %copy-start.4) | copy-done | bytes 196632
  3.5 0.0 copy-start.1
  3.6 0.6 shard_map.77
  4.2 0.5 collective-permute-start
  4.7 2.9 %collective-permute-start.1 = (f32[80,128]{1,0:T(8,128)S(1)}, f32[80,128]{1,0:T(8,128)S(1)}, u32[]{:S(2)}, u32[]{:S(2)}) collective-permute-start(f32[80,128]{1,0:T(8,128)S(1)} %get-tuple-element.16), channel_id=1, source_target_pairs={{0,28},{4,0},{8,4},{12,8},{16,12},{20,16},{24,20},{28,24},{1,29},{... | collective-permute-start | bytes 122888 | tf_op jit(solution)/shard_map/ppermute | solution.py:409
  7.6 0.8 %collective-permute-start.4 = (f32[8,128]{1,0:T(8,128)S(1)}, f32[8,128]{1,0:T(8,128)S(1)}, u32[]{:S(2)}, u32[]{:S(2)}) collective-permute-start(f32[8,128]{1,0:T(8,128)S(1)} %get-tuple-element.19), channel_id=1, source_target_pairs={{0,5},{1,6},{2,7},{3,4},{4,9},{5,10},{6,11},{7,8},{8,13},{9,14},{1... | collective-permute-start | bytes 12296 | tf_op jit(solution)/shard_map/ppermute | solution.py:412
  8.4 3.4 %collective-permute-start.5 = (f32[8,128]{1,0:T(8,128)S(1)}, f32[8,128]{1,0:T(8,128)S(1)}, u32[]{:S(2)}, u32[]{:S(2)}) collective-permute-start(f32[8,128]{1,0:T(8,128)S(1)} %get-tuple-element.20), channel_id=1, source_target_pairs={{0,7},{1,4},{2,5},{3,6},{4,11},{5,8},{6,9},{7,10},{8,15},{9,12},{1... | collective-permute-start | bytes 12296 | tf_op jit(solution)/shard_map/ppermute | solution.py:413
  11.9 0.0 collective-permute-start.2
  11.9 2.4 %collective-permute-done.4.refs_7_ = f32[8,128]{1,0:T(8,128)S(1)} collective-permute-done((f32[8,128]{1,0:T(8,128)S(1)}, f32[8,128]{1,0:T(8,128)S(1)}, u32[]{:S(2)}, u32[]{:S(2)}) %collective-permute-start.4) | collective-permute-done | bytes 4128 | tf_op jit(solution)/shard_map/ppermute | solution.py:412
  14.2 2.5 %collective-permute-start.3 = (f32[24,128]{1,0:T(8,128)S(1)}, f32[24,128]{1,0:T(8,128)S(1)}, u32[]{:S(2)}, u32[]{:S(2)}) collective-permute-start(f32[24,128]{1,0:T(8,128)S(1)} %get-tuple-element.18), channel_id=1, source_target_pairs={{0,3},{1,0},{2,1},{3,2},{4,7},{5,4},{6,5},{7,6},{8,11},{9,8},{10,9... | collective-permute-start | bytes 36872 | tf_op jit(solution)/shard_map/ppermute | solution.py:411
  16.7 0.0 collective-permute-done.5.refs_8_
  16.7 0.0 collective-permute-start.6
  16.7 4.8 %collective-permute-done.6.refs_9_ = f32[8,128]{1,0:T(8,128)S(1)} collective-permute-done((f32[8,128]{1,0:T(8,128)S(1)}, f32[8,128]{1,0:T(8,128)S(1)}, u32[]{:S(2)}, u32[]{:S(2)}) %collective-permute-start.6) | collective-permute-done | bytes 4128 | tf_op jit(solution)/shard_map/ppermute | solution.py:414
  21.6 1.3 %collective-permute-start.7 = (f32[8,128]{1,0:T(8,128)S(1)}, f32[8,128]{1,0:T(8,128)S(1)}, u32[]{:S(2)}, u32[]{:S(2)}) collective-permute-start(f32[8,128]{1,0:T(8,128)S(1)} %get-tuple-element.22), channel_id=1, source_target_pairs={{0,31},{1,28},{2,29},{3,30},{4,3},{5,0},{6,1},{7,2},{8,7},{9,4},{1... | collective-permute-start | bytes 12296 | tf_op jit(solution)/shard_map/ppermute | solution.py:415
  22.9 0.0 copy-done.7
  22.9 13.1 %all-gather = s32[4,6,128]{2,1,0:T(8,128)S(1)} all-gather(s32[1,6,128]{2,1,0:T(8,128)S(1)} %bitcast.1), channel_id=1, replica_groups=mesh['sim'=8,'section'=4] {'section'}, dimensions={0}, use_global_device_ids=true | all-gather | bytes 15360 | tf_op jit(solution)/shard_map/all_gather | solution.py:404
  36.0 0.0 collective-permute-done.7.refs_10_
  36.0 0.0 collective-permute-done.2.refs_5_
  36.0 0.0 collective-permute-done.3.refs_6_
  36.1 0.0 collective-permute-done.refs_3_
  36.1 0.0 collective-permute-done.1.refs_4_
  36.1 0.0 copy-done.1
  36.1 0.0 copy-done.3
  36.1 0.0 copy-done.5
  36.1 0.6 copy-done.8
  36.7 0.9 %copy-done.6 = bf16[256,256]{1,0:T(8,128)(2,1)S(1)} copy-done((bf16[256,256]{1,0:T(8,128)(2,1)S(1)}, bf16[256,256]{1,0:T(8,128)(2,1)}, u32[]{:S(2)}) %copy-start.6) | copy-done | bytes 131096
  37.6 6.2 %shard_map.78 = (f32[5,4,24,128]{3,2,1,0:T(8,128)S(1)}, f32[5,4,24,128]{3,2,1,0:T(8,128)S(1)}, f32[5,4,24,128]{3,2,1,0:T(8,128)S(1)}, f32[5,4,24,128]{3,2,1,0:T(8,128)S(1)}, f32[8,128]{1,0:T(8,128)S(1)}) custom-call(f32[4,96,128]{2,1,0:T(8,128)S(1)} %copy-done.3, f32[3,4,96,128]{3,2,1,0:T(8,128)S(1)} %copy-done.1, f32[4,96,128]{2,1,0:T(8,128)S(1)} %copy-done.5, ...), custom_call_target="tpu_custom_call" | custom-call | tf_op jit(solution)/shard_map/pallas_call | solution.py:291
  43.8 0.7 collective-permute-start.8
  44.5 2.4 %collective-permute-start.9 = (f32[5,4,24,128]{3,2,1,0:T(8,128)S(1)}, f32[5,4,24,128]{3,2,1,0:T(8,128)S(1)}, u32[]{:S(2)}, u32[]{:S(2)}) collective-permute-start(f32[5,4,24,128]{3,2,1,0:T(8,128)S(1)} %get-tuple-element.25), channel_id=1, source_target_pairs={{0,2},{1,3},{2,0},{3,1},{4,6},{5,7},{6,4},{7,5},{8,10},{9,11},{10,... | collective-permute-start | bytes 737288 | tf_op jit(solution)/shard_map/ppermute | solution.py:419
  46.9 1.4 %collective-permute-start.10 = (f32[5,4,24,128]{3,2,1,0:T(8,128)S(1)}, f32[5,4,24,128]{3,2,1,0:T(8,128)S(1)}, u32[]{:S(2)}, u32[]{:S(2)}) collective-permute-start(f32[5,4,24,128]{3,2,1,0:T(8,128)S(1)} %get-tuple-element.26), channel_id=1, source_target_pairs={{0,3},{1,2},{2,1},{3,0},{4,7},{5,6},{6,5},{7,4},{8,11},{9,10},{10,... | collective-permute-start | bytes 737288 | tf_op jit(solution)/shard_map/ppermute | solution.py:419
  48.2 0.0 collective-permute-start.11
  48.2 8.2 %collective-permute-done.11 = f32[8,128]{1,0:T(8,128)S(1)} collective-permute-done((f32[8,128]{1,0:T(8,128)S(1)}, f32[8,128]{1,0:T(8,128)S(1)}, u32[]{:S(2)}, u32[]{:S(2)}) %collective-permute-start.11) | collective-permute-done | bytes 4128 | tf_op jit(solution)/shard_map/ppermute | solution.py:396
  56.4 2.8 %collective-permute-start.12 = (f32[8,128]{1,0:T(8,128)S(1)}, f32[8,128]{1,0:T(8,128)S(1)}, u32[]{:S(2)}, u32[]{:S(2)}) collective-permute-start(f32[8,128]{1,0:T(8,128)S(1)} %max.15), channel_id=1, source_target_pairs={{0,2},{1,3},{2,0},{3,1},{4,6},{5,7},{6,4},{7,5},{8,10},{9,11},{10,... | collective-permute-start | bytes 12296 | tf_op jit(solution)/shard_map/ppermute | solution.py:396
  59.2 5.8 %collective-permute-done.12 = f32[8,128]{1,0:T(8,128)S(1)} collective-permute-done((f32[8,128]{1,0:T(8,128)S(1)}, f32[8,128]{1,0:T(8,128)S(1)}, u32[]{:S(2)}, u32[]{:S(2)}) %collective-permute-start.12) | collective-permute-done | bytes 4128 | tf_op jit(solution)/shard_map/ppermute | solution.py:396
  64.9 0.0 collective-permute-start.13
  64.9 1.2 %collective-permute-done.13 = f32[8,128]{1,0:T(8,128)S(1)} collective-permute-done((f32[8,128]{1,0:T(8,128)S(1)}, f32[8,128]{1,0:T(8,128)S(1)}, u32[]{:S(2)}, u32[]{:S(2)}) %collective-permute-start.13) | collective-permute-done | bytes 4128 | tf_op jit(solution)/shard_map/ppermute | solution.py:396
  66.1 2.3 %collective-permute-start.14 = (f32[8,128]{1,0:T(8,128)S(1)}, f32[8,128]{1,0:T(8,128)S(1)}, u32[]{:S(2)}, u32[]{:S(2)}) collective-permute-start(f32[8,128]{1,0:T(8,128)S(1)} %max.17), channel_id=1, source_target_pairs={{0,8},{4,12},{8,0},{12,4},{16,24},{20,28},{24,16},{28,20},{1,9},{5... | collective-permute-start | bytes 12296 | tf_op jit(solution)/shard_map/ppermute | solution.py:396
  68.4 1.6 %collective-permute-done.14 = f32[8,128]{1,0:T(8,128)S(1)} collective-permute-done((f32[8,128]{1,0:T(8,128)S(1)}, f32[8,128]{1,0:T(8,128)S(1)}, u32[]{:S(2)}, u32[]{:S(2)}) %collective-permute-start.14) | collective-permute-done | bytes 4128 | tf_op jit(solution)/shard_map/ppermute | solution.py:396
  70.0 1.2 %collective-permute-start.15 = (f32[8,128]{1,0:T(8,128)S(1)}, f32[8,128]{1,0:T(8,128)S(1)}, u32[]{:S(2)}, u32[]{:S(2)}) collective-permute-start(f32[8,128]{1,0:T(8,128)S(1)} %max.18), channel_id=1, source_target_pairs={{0,16},{4,20},{8,24},{12,28},{16,0},{20,4},{24,8},{28,12},{1,17},{... | collective-permute-start | bytes 12296 | tf_op jit(solution)/shard_map/ppermute | solution.py:396
  71.2 2.4 %collective-permute-done.15 = f32[8,128]{1,0:T(8,128)S(1)} collective-permute-done((f32[8,128]{1,0:T(8,128)S(1)}, f32[8,128]{1,0:T(8,128)S(1)}, u32[]{:S(2)}, u32[]{:S(2)}) %collective-permute-start.15) | collective-permute-done | bytes 4128 | tf_op jit(solution)/shard_map/ppermute | solution.py:396
  73.6 0.0 collective-permute-done.8.refs_1_
  73.6 0.0 collective-permute-done.9.refs_2_
  73.6 0.0 collective-permute-done.10.refs_3_
  73.7 1.8 %shard_map.79 = (f32[5,4,24,512]{3,2,1,0:T(8,128)}, f32[5,64]{1,0:T(8,128)}) custom-call(f32[5,4,24,128]{3,2,1,0:T(8,128)S(1)} %get-tuple-element.23.refs_0_, f32[5,4,24,128]{3,2,1,0:T(8,128)S(1)} %collective-permute-done.8.refs_1_, f32[5,4,24,128]{3,2,1,0:T(8,128)S(1)} %collective-permute-done.9.refs_2_, ...), custom_call_target="tpu_custom_call" | custom-call | tf_op jit(solution)/shard_map/pallas_call | solution.py:355
  (12 shorter events, 0.0 us)
Async XLA Ops:
  0.6 1.1 %copy-start = (f32[3,4,96,128]{3,2,1,0:T(8,128)S(1)}, f32[3,4,96,128]{3,2,1,0:T(8,128)}, u32[]{:S(2)}) copy-start(f32[3,4,96,128]{3,2,1,0:T(8,128)} %refs_1_.1) | copy-start | bytes 1769476
  1.7 0.9 %copy-start.2 = (f32[4,96,128]{2,1,0:T(8,128)S(1)}, f32[4,96,128]{2,1,0:T(8,128)}, u32[]{:S(2)}) copy-start(f32[4,96,128]{2,1,0:T(8,128)} %refs_0_.1) | copy-start | bytes 589828
  2.6 0.9 %copy-start.4 = (f32[4,96,128]{2,1,0:T(8,128)S(1)}, f32[4,96,128]{2,1,0:T(8,128)}, u32[]{:S(2)}) copy-start(f32[4,96,128]{2,1,0:T(8,128)} %refs_2_.1) | copy-start | bytes 589828
  3.5 32.5 %copy-start.1 = (f32[3,4,96,128]{3,2,1,0:T(8,128)S(1)}, f32[3,4,96,128]{3,2,1,0:T(8,128)}, u32[]{:S(2)}) copy-start(f32[3,4,96,128]{3,2,1,0:T(8,128)} %refs_1_.1) | copy-start | bytes 1769476
  3.6 32.5 %copy-start.3 = (f32[4,96,128]{2,1,0:T(8,128)S(1)}, f32[4,96,128]{2,1,0:T(8,128)}, u32[]{:S(2)}) copy-start(f32[4,96,128]{2,1,0:T(8,128)} %refs_0_.1) | copy-start | bytes 589828
  3.6 32.5 %copy-start.5 = (f32[4,96,128]{2,1,0:T(8,128)S(1)}, f32[4,96,128]{2,1,0:T(8,128)}, u32[]{:S(2)}) copy-start(f32[4,96,128]{2,1,0:T(8,128)} %refs_2_.1) | copy-start | bytes 589828
  4.2 31.9 %collective-permute-start = (f32[80,128]{1,0:T(8,128)S(1)}, f32[80,128]{1,0:T(8,128)S(1)}, u32[]{:S(2)}, u32[]{:S(2)}) collective-permute-start(f32[80,128]{1,0:T(8,128)S(1)} %get-tuple-element.15), channel_id=1, source_target_pairs={{0,4},{4,8},{8,12},{12,16},{16,20},{20,24},{24,28},{28,0},{1,5},{5... | collective-permute-start | bytes 122888 | tf_op jit(solution)/shard_map/ppermute | solution.py:408
  4.7 31.4 %collective-permute-start.1 = (f32[80,128]{1,0:T(8,128)S(1)}, f32[80,128]{1,0:T(8,128)S(1)}, u32[]{:S(2)}, u32[]{:S(2)}) collective-permute-start(f32[80,128]{1,0:T(8,128)S(1)} %get-tuple-element.16), channel_id=1, source_target_pairs={{0,28},{4,0},{8,4},{12,8},{16,12},{20,16},{24,20},{28,24},{1,29},{... | collective-permute-start | bytes 122888 | tf_op jit(solution)/shard_map/ppermute | solution.py:409
  7.6 6.6 %collective-permute-start.4 = (f32[8,128]{1,0:T(8,128)S(1)}, f32[8,128]{1,0:T(8,128)S(1)}, u32[]{:S(2)}, u32[]{:S(2)}) collective-permute-start(f32[8,128]{1,0:T(8,128)S(1)} %get-tuple-element.19), channel_id=1, source_target_pairs={{0,5},{1,6},{2,7},{3,4},{4,9},{5,10},{6,11},{7,8},{8,13},{9,14},{1... | collective-permute-start | bytes 12296 | tf_op jit(solution)/shard_map/ppermute | solution.py:412
  8.4 8.3 %collective-permute-start.5 = (f32[8,128]{1,0:T(8,128)S(1)}, f32[8,128]{1,0:T(8,128)S(1)}, u32[]{:S(2)}, u32[]{:S(2)}) collective-permute-start(f32[8,128]{1,0:T(8,128)S(1)} %get-tuple-element.20), channel_id=1, source_target_pairs={{0,7},{1,4},{2,5},{3,6},{4,11},{5,8},{6,9},{7,10},{8,15},{9,12},{1... | collective-permute-start | bytes 12296 | tf_op jit(solution)/shard_map/ppermute | solution.py:413
  11.9 11.0 %copy-start.7 = (s32[6,128]{1,0:T(8,128)S(1)}, s32[6,128]{1,0:T(8,128)}, u32[]{:S(2)}) copy-start(s32[6,128]{1,0:T(8,128)} %refs_5_.1) | copy-start | bytes 9220
  11.9 24.2 %collective-permute-start.2 = (f32[24,128]{1,0:T(8,128)S(1)}, f32[24,128]{1,0:T(8,128)S(1)}, u32[]{:S(2)}, u32[]{:S(2)}) collective-permute-start(f32[24,128]{1,0:T(8,128)S(1)} %get-tuple-element.17), channel_id=1, source_target_pairs={{0,1},{1,2},{2,3},{3,0},{4,5},{5,6},{6,7},{7,4},{8,9},{9,10},{10,1... | collective-permute-start | bytes 36872 | tf_op jit(solution)/shard_map/ppermute | solution.py:410
  14.2 21.8 %collective-permute-start.3 = (f32[24,128]{1,0:T(8,128)S(1)}, f32[24,128]{1,0:T(8,128)S(1)}, u32[]{:S(2)}, u32[]{:S(2)}) collective-permute-start(f32[24,128]{1,0:T(8,128)S(1)} %get-tuple-element.18), channel_id=1, source_target_pairs={{0,3},{1,0},{2,1},{3,2},{4,7},{5,4},{6,5},{7,6},{8,11},{9,8},{10,9... | collective-permute-start | bytes 36872 | tf_op jit(solution)/shard_map/ppermute | solution.py:411
  16.7 4.8 %collective-permute-start.6 = (f32[8,128]{1,0:T(8,128)S(1)}, f32[8,128]{1,0:T(8,128)S(1)}, u32[]{:S(2)}, u32[]{:S(2)}) collective-permute-start(f32[8,128]{1,0:T(8,128)S(1)} %get-tuple-element.21), channel_id=1, source_target_pairs={{0,29},{1,30},{2,31},{3,28},{4,1},{5,2},{6,3},{7,0},{8,5},{9,6},{1... | collective-permute-start | bytes 12296 | tf_op jit(solution)/shard_map/ppermute | solution.py:414
  21.6 14.5 %collective-permute-start.7 = (f32[8,128]{1,0:T(8,128)S(1)}, f32[8,128]{1,0:T(8,128)S(1)}, u32[]{:S(2)}, u32[]{:S(2)}) collective-permute-start(f32[8,128]{1,0:T(8,128)S(1)} %get-tuple-element.22), channel_id=1, source_target_pairs={{0,31},{1,28},{2,29},{3,30},{4,3},{5,0},{6,1},{7,2},{8,7},{9,4},{1... | collective-permute-start | bytes 12296 | tf_op jit(solution)/shard_map/ppermute | solution.py:415
  36.0 0.7 copy-start.8
  36.7 0.9 %copy-start.6 = (bf16[256,256]{1,0:T(8,128)(2,1)S(1)}, bf16[256,256]{1,0:T(8,128)(2,1)}, u32[]{:S(2)}) copy-start(bf16[256,256]{1,0:T(8,128)(2,1)} %constant.2.clone.refs_13_) | copy-start | bytes 393220
  43.8 29.9 %collective-permute-start.8 = (f32[5,4,24,128]{3,2,1,0:T(8,128)S(1)}, f32[5,4,24,128]{3,2,1,0:T(8,128)S(1)}, u32[]{:S(2)}, u32[]{:S(2)}) collective-permute-start(f32[5,4,24,128]{3,2,1,0:T(8,128)S(1)} %get-tuple-element.24), channel_id=1, source_target_pairs={{0,1},{1,0},{2,3},{3,2},{4,5},{5,4},{6,7},{7,6},{8,9},{9,8},{10,11... | collective-permute-start | bytes 737288 | tf_op jit(solution)/shard_map/ppermute | solution.py:419
  44.5 29.1 %collective-permute-start.9 = (f32[5,4,24,128]{3,2,1,0:T(8,128)S(1)}, f32[5,4,24,128]{3,2,1,0:T(8,128)S(1)}, u32[]{:S(2)}, u32[]{:S(2)}) collective-permute-start(f32[5,4,24,128]{3,2,1,0:T(8,128)S(1)} %get-tuple-element.25), channel_id=1, source_target_pairs={{0,2},{1,3},{2,0},{3,1},{4,6},{5,7},{6,4},{7,5},{8,10},{9,11},{10,... | collective-permute-start | bytes 737288 | tf_op jit(solution)/shard_map/ppermute | solution.py:419
  46.9 26.8 %collective-permute-start.10 = (f32[5,4,24,128]{3,2,1,0:T(8,128)S(1)}, f32[5,4,24,128]{3,2,1,0:T(8,128)S(1)}, u32[]{:S(2)}, u32[]{:S(2)}) collective-permute-start(f32[5,4,24,128]{3,2,1,0:T(8,128)S(1)} %get-tuple-element.26), channel_id=1, source_target_pairs={{0,3},{1,2},{2,1},{3,0},{4,7},{5,6},{6,5},{7,4},{8,11},{9,10},{10,... | collective-permute-start | bytes 737288 | tf_op jit(solution)/shard_map/ppermute | solution.py:419
  48.2 8.2 %collective-permute-start.11 = (f32[8,128]{1,0:T(8,128)S(1)}, f32[8,128]{1,0:T(8,128)S(1)}, u32[]{:S(2)}, u32[]{:S(2)}) collective-permute-start(f32[8,128]{1,0:T(8,128)S(1)} %get-tuple-element.27), channel_id=1, source_target_pairs={{0,1},{1,0},{2,3},{3,2},{4,5},{5,4},{6,7},{7,6},{8,9},{9,8},{10,11... | collective-permute-start | bytes 12296 | tf_op jit(solution)/shard_map/ppermute | solution.py:396
  56.4 8.5 %collective-permute-start.12 = (f32[8,128]{1,0:T(8,128)S(1)}, f32[8,128]{1,0:T(8,128)S(1)}, u32[]{:S(2)}, u32[]{:S(2)}) collective-permute-start(f32[8,128]{1,0:T(8,128)S(1)} %max.15), channel_id=1, source_target_pairs={{0,2},{1,3},{2,0},{3,1},{4,6},{5,7},{6,4},{7,5},{8,10},{9,11},{10,... | collective-permute-start | bytes 12296 | tf_op jit(solution)/shard_map/ppermute | solution.py:396
  64.9 1.2 %collective-permute-start.13 = (f32[8,128]{1,0:T(8,128)S(1)}, f32[8,128]{1,0:T(8,128)S(1)}, u32[]{:S(2)}, u32[]{:S(2)}) collective-permute-start(f32[8,128]{1,0:T(8,128)S(1)} %max.16), channel_id=1, source_target_pairs={{0,4},{4,0},{8,12},{12,8},{16,20},{20,16},{24,28},{28,24},{1,5},{5... | collective-permute-start | bytes 12296 | tf_op jit(solution)/shard_map/ppermute | solution.py:396
  66.1 3.9 %collective-permute-start.14 = (f32[8,128]{1,0:T(8,128)S(1)}, f32[8,128]{1,0:T(8,128)S(1)}, u32[]{:S(2)}, u32[]{:S(2)}) collective-permute-start(f32[8,128]{1,0:T(8,128)S(1)} %max.17), channel_id=1, source_target_pairs={{0,8},{4,12},{8,0},{12,4},{16,24},{20,28},{24,16},{28,20},{1,9},{5... | collective-permute-start | bytes 12296 | tf_op jit(solution)/shard_map/ppermute | solution.py:396
  70.0 3.6 %collective-permute-start.15 = (f32[8,128]{1,0:T(8,128)S(1)}, f32[8,128]{1,0:T(8,128)S(1)}, u32[]{:S(2)}, u32[]{:S(2)}) collective-permute-start(f32[8,128]{1,0:T(8,128)S(1)} %max.18), channel_id=1, source_target_pairs={{0,16},{4,20},{8,24},{12,28},{16,0},{20,4},{24,8},{28,12},{1,17},{... | collective-permute-start | bytes 12296 | tf_op jit(solution)/shard_map/ppermute | solution.py:396
